TPU v7x, 768 devices: a whole 4x8x12 slice. The times are simulated.
768 devices in a mesh: comp: 8 (over y_hi, core), tile: 96 (over y_lo, x, z).
Axes of the slice: x: 4, y: 8 (y_hi: 4, y_lo: 2; y = y_hi * 2 + y_lo), z: 12, core: 2. Of those that a mesh axis runs over, the one named last changes fastest.
Arguments:
- state: float32 [8, 2, 48, 1536, 256], P('comp', None, None, 'tile'), may hold values from -6 to 6
- kappa: float32 [8, 1536, 256], P('comp', 'tile'), may hold values from 0.05 to 0.22
- forcing: float32 [8, 12, 1536, 256], P('comp', None, 'tile'), may hold values from -6 to 6
- flux_gain: float32 [8, 12], P('comp'), may hold values from -4 to 4
- src_index: int32 [8, 96, 5, 256], P('comp', 'tile'), may hold values from 0 to 4095
- intersection: float32 [8, 96, 5, 256], P('comp', 'tile'), may hold values from 0.1 to 1
- pair_count: int32 [8, 96, 5], P('comp', 'tile'), may hold values from 1 to 256, 640 in all within a row
- dst_index: int32 [8, 96, 5, 256], P('comp', 'tile'), may hold values from 0 to 4095
- cell_area: float32 [8, 1536, 256], P('comp', 'tile'), may hold values from 0.5 to 2
Outputs:
- state_out: float32 [8, 2, 48, 1536, 256], P('comp', None, None, 'tile')
- remapped: float32 [8, 12, 1536, 256], P('comp', None, 'tile')
Inputs may be any that keep to these rules, and one draw needn't show every extreme that they name: `pair_count`: for every sending device the counts over its 5 partner blocks sum to 640, and one of them is exactly 256.
All inputs are finite; a program needn't handle non-finite values.
Results may differ from a plain program's by a relative error of at most 0.0029.
Values may be sent and summed in bfloat16 or wider, within the bound.
A program may use at most 32 MiB of HBM per device.

v0:
```python
import jax
import jax.numpy as jnp
from jax import lax
from jax.sharding import PartitionSpec as P

NF = 12


def extended(cells, sides, width):
    for axis, dim in sides:
        count = lax.axis_size(axis)
        head = lax.slice_in_dim(cells, 0, width, axis=dim)
        tail = lax.slice_in_dim(cells, cells.shape[dim] - width, cells.shape[dim], axis=dim)
        cells = jnp.concatenate(
            [
                lax.ppermute(tail, axis, [(i, (i + 1) % count) for i in range(count)]),
                cells,
                lax.ppermute(head, axis, [((i + 1) % count, i) for i in range(count)]),
            ],
            axis=dim,
        )
    return cells


def passed_along(shard, axis, by):
    length = lax.axis_size(axis)
    return lax.ppermute(shard, axis, [(i, (i + by) % length) for i in range(length)])


def partner(shard, axis, distance):
    return lax.ppermute(shard, axis, [(i, i ^ 1 << distance) for i in range(lax.axis_size(axis))])


def advance(padded, coef):
    center = padded[:, 1:-1]
    right = jnp.roll(center, -1, axis=2)
    left = jnp.roll(center, 1, axis=2)
    lap = padded[:, 2:] + padded[:, :-2] + right + left - 4.0 * center
    return center + coef[None] * lap


def local(
    state, kappa, forcing, flux_gain, src_index, intersection, pair_count, dst_index, cell_area
):
    nvars, levels, rows, cols = (state.shape[1], state.shape[2], state.shape[3], state.shape[4])
    entries = src_index.shape[2]
    slots = src_index.shape[3]
    cells = rows * cols
    fields = state[0].reshape(nvars * levels, rows, cols)
    coef = kappa[0]
    for step in range(2):
        padded = extended(fields, (("tile", 1),), 1)
        fields = advance(padded, coef)
    state_out = fields.reshape(1, nvars, levels, rows, cols)
    surface = state[0][:, 0]
    chosen = jnp.tile(surface, (NF // 2, 1, 1))
    flux = (forcing[0] + flux_gain[0][:, None, None] * chosen).reshape(NF, cells)
    picked = jnp.take(flux, src_index[0, 0].reshape(-1), axis=1).reshape(NF, entries, slots)
    live = jnp.arange(slots, dtype=jnp.int32)[None, :] < pair_count[0, 0][:, None]
    weight = jnp.where(live, intersection[0, 0], jnp.float32(0.0))
    outgoing = (weight[None] * picked).astype(jnp.bfloat16)
    outgoing = outgoing.transpose(1, 0, 2).reshape(entries, NF * slots)
    partner_bit = lax.axis_size("comp").bit_length() - 2
    pieces = []
    for entry in range(entries):
        offset = entry - entries // 2
        if offset == 0:
            pieces.append(outgoing[entry])
        else:
            pieces.append(passed_along(outgoing[entry], "tile", offset))
    moved = jnp.stack(pieces, axis=0)
    incoming = partner(moved, "comp", partner_bit)
    values = incoming.reshape(entries, NF, slots).transpose(0, 2, 1).reshape(entries * slots, NF)
    total = jnp.zeros((cells, NF), jnp.float32)
    total = total.at[dst_index[0, 0].reshape(-1)].add(values.astype(jnp.float32))
    remapped = total.T.reshape(NF, rows, cols) / cell_area[0][None]
    return (state_out, remapped[None])


def solution(mesh):
    return jax.shard_map(
        local,
        mesh=mesh,
        in_specs=(
            P("comp", None, None, "tile", None),
            P("comp", "tile", None),
            P("comp", None, "tile", None),
            P("comp", None),
            P("comp", "tile", None, None),
            P("comp", "tile", None, None),
            P("comp", "tile", None),
            P("comp", "tile", None, None),
            P("comp", "tile", None),
        ),
        out_specs=(P("comp", None, None, "tile", None), P("comp", None, "tile", None)),
        check_vma=False,
    )
```

profile of v0, /device:TPU:40, one launch (start us, length us, event | category | flops | bytes accessed | tf_op | source)
XLA Modules:
  0.0 100.4 jit_solution(11004239314731110244)
XLA Ops:
  0.6 2.2 %fusion.22 = (f32[96,1,256]{2,1,0:T(1,128)}, f32[96,1,256]{2,1,0:T(1,128)}) fusion(f32[96,16,256]{2,1,0:T(8,128)} %bitcast.40), kind=kLoop, calls=%fused_computation.41 | loop fusion | bytes 393216 | tf_op jit(solution)/shard_map/slice | solution.py:12
  2.8 17.6 %collective-permute-start = (f32[96,1,256]{2,1,0:T(1,128)}, f32[96,1,256]{2,1,0:T(1,128)S(1)}, u32[]{:S(2)}, u32[]{:S(2)}) collective-permute-start(f32[96,1,256]{2,1,0:T(1,128)} %get-tuple-element.12), channel_id=1, source_target_pairs={{1,0},{2,1},{3,2},{4,3},{5,4},{6,5},{7,6},{8,7},{9,8},{10,9},{11,1... | collective-permute-start | bytes 294920 | tf_op jit(solution)/shard_map/ppermute | solution.py:18
  22.1 2.0 %copy.13 = f32[1,12,16,256]{1,3,2,0:T(8,128)} copy(f32[1,12,16,256]{3,2,1,0:T(8,128)S(1)} %copy-done.1) | data formatting | bytes 393216 | tf_op args[2]
  24.2 3.1 %bitcast_add_fusion = f32[12,4096]{0,1:T(8,128)} fusion(f32[1,12,16,256]{1,3,2,0:T(8,128)} %copy.13, f32[12,4096]{0,1:T(8,128)S(1)} %copy.14, f32[12]{0:T(128)S(1)} %bitcast.59), kind=kLoop, calls=%fused_computation.2 | loop fusion | flops 98304 | bytes 589872 | tf_op jit(solution)/shard_map/add | solution.py:57
  27.3 4.1 %gather_fusion = f32[1280,12]{1,0:T(8,128)S(1)} fusion(f32[12,4096]{0,1:T(8,128)} %bitcast_add_fusion, s32[2048]{0:T(1024)S(1)} %pad_clamp_fusion), kind=kCustom, calls=%fused_computation | custom fusion | bytes 128000 | tf_op jit(solution)/shard_map/jit(_take)/gather | solution.py:58
  31.7 2.5 %collective-permute-start.4 = (bf16[3072]{0:T(1024)(128)(2,1)S(1)}, bf16[3072]{0:T(1024)(128)(2,1)S(1)}, u32[]{:S(2)}, u32[]{:S(2)}) collective-permute-start(bf16[3072]{0:T(1024)(128)(2,1)S(1)} %squeeze.24), channel_id=1, source_target_pairs={{0,94},{1,95},{2,0},{3,1},{4,2},{5,3},{6,4},{7,5},{8,6},{9,7},{10,... | collective-permute-start | bytes 18440 | tf_op jit(solution)/shard_map/ppermute | solution.py:27
  34.2 2.5 %collective-permute-start.5 = (bf16[3072]{0:T(1024)(128)(2,1)S(1)}, bf16[3072]{0:T(1024)(128)(2,1)S(1)}, u32[]{:S(2)}, u32[]{:S(2)}) collective-permute-start(bf16[3072]{0:T(1024)(128)(2,1)S(1)} %squeeze.25), channel_id=1, source_target_pairs={{0,95},{1,0},{2,1},{3,2},{4,3},{5,4},{6,5},{7,6},{8,7},{9,8},{10,9... | collective-permute-start | bytes 18440 | tf_op jit(solution)/shard_map/ppermute | solution.py:27
  36.7 3.4 %collective-permute-start.6 = (bf16[3072]{0:T(1024)(128)(2,1)S(1)}, bf16[3072]{0:T(1024)(128)(2,1)S(1)}, u32[]{:S(2)}, u32[]{:S(2)}) collective-permute-start(bf16[3072]{0:T(1024)(128)(2,1)S(1)} %squeeze.26), channel_id=1, source_target_pairs={{0,1},{1,2},{2,3},{3,4},{4,5},{5,6},{6,7},{7,8},{8,9},{9,10},{10,1... | collective-permute-start | bytes 18440 | tf_op jit(solution)/shard_map/ppermute | solution.py:27
  40.1 4.3 %collective-permute-start.7 = (bf16[3072]{0:T(1024)(128)(2,1)S(1)}, bf16[3072]{0:T(1024)(128)(2,1)S(1)}, u32[]{:S(2)}, u32[]{:S(2)}) collective-permute-start(bf16[3072]{0:T(1024)(128)(2,1)S(1)} %squeeze.27), channel_id=1, source_target_pairs={{0,2},{1,3},{2,4},{3,5},{4,6},{5,7},{6,8},{7,9},{8,10},{9,11},{10,... | collective-permute-start | bytes 18440 | tf_op jit(solution)/shard_map/ppermute | solution.py:27
  44.4 1.7 %fusion.21 = (f32[96,16,255]{2,1,0:T(8,128)S(1)}, f32[96,16,255]{2,1,0:T(8,128)}) fusion(f32[96,16,256]{2,1,0:T(8,128)S(1)} %bitcast.42), kind=kLoop, calls=%fused_computation.40 | loop fusion | bytes 6266880 | tf_op jit(solution)/shard_map/jit(_roll_static)/slice | solution.py:37
  46.2 1.4 %fusion.20 = (f32[96,16,1]{2,1,0:T(8,128)}, f32[96,16,1]{2,1,0:T(8,128)}) fusion(f32[96,16,256]{2,1,0:T(8,128)S(1)} %bitcast.43), kind=kLoop, calls=%fused_computation.39 | loop fusion | bytes 24576 | tf_op jit(solution)/shard_map/jit(_roll_static)/slice | solution.py:37
  47.6 1.9 %collective-permute-start.1 = (f32[96,1,256]{2,1,0:T(1,128)}, f32[96,1,256]{2,1,0:T(1,128)S(1)}, u32[]{:S(2)}, u32[]{:S(2)}) collective-permute-start(f32[96,1,256]{2,1,0:T(1,128)} %get-tuple-element.13), channel_id=1, source_target_pairs={{0,1},{1,2},{2,3},{3,4},{4,5},{5,6},{6,7},{7,8},{8,9},{9,10},{10,1... | collective-permute-start | bytes 294920 | tf_op jit(solution)/shard_map/ppermute | solution.py:16
  49.6 1.3 %collective-permute-done.7 = bf16[3072]{0:T(1024)(128)(2,1)S(1)} collective-permute-done((bf16[3072]{0:T(1024)(128)(2,1)S(1)}, bf16[3072]{0:T(1024)(128)(2,1)S(1)}, u32[]{:S(2)}, u32[]{:S(2)}) %collective-permute-start.7) | collective-permute-done | bytes 6176 | tf_op jit(solution)/shard_map/ppermute | solution.py:27
  50.9 2.0 %collective-permute-start.8 = (bf16[5,3072]{1,0:T(8,128)(2,1)S(1)}, bf16[5,3072]{1,0:T(8,128)(2,1)S(1)}, u32[]{:S(2)}, u32[]{:S(2)}) collective-permute-start(bf16[5,3072]{1,0:T(8,128)(2,1)S(1)} %stack.19), channel_id=1, source_target_pairs={{0,384},{96,480},{192,576},{288,672},{384,0},{480,96},{576,192},{6... | collective-permute-start | bytes 92168 | tf_op jit(solution)/shard_map/ppermute | solution.py:31
  53.0 8.4 %collective-permute-done.8 = bf16[5,3072]{1,0:T(8,128)(2,1)S(1)} collective-permute-done((bf16[5,3072]{1,0:T(8,128)(2,1)S(1)}, bf16[5,3072]{1,0:T(8,128)(2,1)S(1)}, u32[]{:S(2)}, u32[]{:S(2)}) %collective-permute-start.8) | collective-permute-done | bytes 30752 | tf_op jit(solution)/shard_map/ppermute | solution.py:31
  61.4 1.1 %copy.19 = f32[5,256,12]{2,1,0:T(8,128)} copy(f32[5,256,12]{1,0,2:T(8,128)S(1)} %convert_bitcast_fusion) | data formatting | bytes 122880 | tf_op jit(solution)/shard_map/convert_element_type | solution.py:75
  62.5 10.6 %scatter_custom_fusion = f32[4096,12]{1,0:T(8,128)} fusion(s32[1280]{0:T(1024)S(1)} %fusion.15, f32[1280,12]{1,0:T(8,128)} %bitcast.51, f32[]{:T(128)} %constant.7.clone.1), kind=kCustom, calls=%fused_computation.19 | custom fusion | flops 15360 | bytes 197120 | tf_op jit(solution)/shard_map/scatter-add | solution.py:75
  73.0 2.2 %copy.18 = f32[1,12,16,256]{3,2,1,0:T(8,128)S(1)} copy(f32[1,12,16,256]{1,3,2,0:T(8,128)} %bitcast.45) | data formatting | bytes 393216 | tf_op jit(solution)/shard_map/reshape | solution.py:76
  75.3 1.4 %broadcast_divide_fusion = f32[1,12,16,256]{3,2,1,0:T(8,128)} fusion(f32[1,12,16,256]{3,2,1,0:T(8,128)S(1)} %copy.18, f32[16,256]{1,0:T(8,128)} %bitcast.57), kind=kLoop, calls=%fused_computation.22 | loop fusion | flops 49152 | bytes 409600 | tf_op jit(solution)/shard_map/div | solution.py:76
  76.7 3.0 %fusion.11 = f32[96,16,256]{2,1,0:T(8,128)S(1)} fusion(f32[96,16,256]{2,1,0:T(8,128)S(1)} %bitcast.44, f32[96,1,256]{2,1,0:T(1,128)S(1)} %collective-permute-done.1, f32[96,1,256]{2,1,0:T(1,128)S(1)} %collective-permute-done, f32[96,16,1]{2,1,0:T(8,128)} %get-tuple-element.9, f32[96,16,255]{2,1,0:T(8,128)} %get-tuple-element.11, ...), kind=kLoop, calls=%fused_computation.17 | loop fusion | flops 4325376 | bytes 6504448 | tf_op jit(solution)/shard_map/add | solution.py:39
  80.4 6.9 %collective-permute-start.2 = (f32[96,1,256]{2,1,0:T(1,128)S(1)}, f32[96,1,256]{2,1,0:T(1,128)S(1)}, u32[]{:S(2)}, u32[]{:S(2)}) collective-permute-start(f32[96,1,256]{2,1,0:T(1,128)S(1)} %get-tuple-element.6), channel_id=1, source_target_pairs={{1,0},{2,1},{3,2},{4,3},{5,4},{6,5},{7,6},{8,7},{9,8},{10,9},{11,1... | collective-permute-start | bytes 294920 | tf_op jit(solution)/shard_map/ppermute | solution.py:18
  87.3 1.9 %collective-permute-start.3 = (f32[96,1,256]{2,1,0:T(1,128)S(1)}, f32[96,1,256]{2,1,0:T(1,128)S(1)}, u32[]{:S(2)}, u32[]{:S(2)}) collective-permute-start(f32[96,1,256]{2,1,0:T(1,128)S(1)} %get-tuple-element.7), channel_id=1, source_target_pairs={{0,1},{1,2},{2,3},{3,4},{4,5},{5,6},{6,7},{7,8},{8,9},{9,10},{10,1... | collective-permute-start | bytes 294920 | tf_op jit(solution)/shard_map/ppermute | solution.py:16
  89.5 8.5 %collective-permute-done.3 = f32[96,1,256]{2,1,0:T(1,128)S(1)} collective-permute-done((f32[96,1,256]{2,1,0:T(1,128)S(1)}, f32[96,1,256]{2,1,0:T(1,128)S(1)}, u32[]{:S(2)}, u32[]{:S(2)}) %collective-permute-start.3) | collective-permute-done | bytes 98336 | tf_op jit(solution)/shard_map/ppermute | solution.py:16
  98.0 2.4 %fusion.5 = f32[96,16,256]{2,1,0:T(8,128)} fusion(f32[96,16,256]{2,1,0:T(8,128)S(1)} %fusion.11, f32[96,1,256]{2,1,0:T(1,128)S(1)} %collective-permute-done.3, f32[96,1,256]{2,1,0:T(1,128)S(1)} %collective-permute-done.2, f32[96,16,1]{2,1,0:T(8,128)S(1)} %get-tuple-element.3, f32[96,16,255]{2,1,0:T(8,128)S(1)} %get-tuple-element.5, ...), kind=kLoop, calls=%fused_computation.9 | loop fusion | flops 4325376 | bytes 6504448 | tf_op jit(solution)/shard_map/add | solution.py:39
  (49 shorter events, 3.3 us)
Async XLA Ops:
  2.8 73.9 %collective-permute-start = (f32[96,1,256]{2,1,0:T(1,128)}, f32[96,1,256]{2,1,0:T(1,128)S(1)}, u32[]{:S(2)}, u32[]{:S(2)}) collective-permute-start(f32[96,1,256]{2,1,0:T(1,128)} %get-tuple-element.12), channel_id=1, source_target_pairs={{1,0},{2,1},{3,2},{4,3},{5,4},{6,5},{7,6},{8,7},{9,8},{10,9},{11,1... | collective-permute-start | bytes 294920 | tf_op jit(solution)/shard_map/ppermute | solution.py:18
  21.2 0.9 copy-start.1
  22.1 2.0 %copy-start.3 = (s32[1,1,5,256]{3,1,2,0:T(1,128)S(1)}, s32[1,1,5,256]{3,1,2,0:T(1,128)}, u32[]{:S(2)}) copy-start(s32[1,1,5,256]{3,1,2,0:T(1,128)} %param.13) | copy-start | bytes 15364
  22.1 2.1 %copy-start.6 = (f32[1,12]{1,0:T(1,128)S(1)}, f32[1,12]{1,0:T(1,128)}, u32[]{:S(2)}) copy-start(f32[1,12]{1,0:T(1,128)} %param.12) | copy-start | bytes 148
  24.2 7.4 %copy-start.4 = (f32[1,1,5,256]{3,1,2,0:T(1,128)S(1)}, f32[1,1,5,256]{3,1,2,0:T(1,128)}, u32[]{:S(2)}) copy-start(f32[1,1,5,256]{3,1,2,0:T(1,128)} %param.14) | copy-start | bytes 15364
  24.2 7.4 %copy-start.7 = (s32[1,1,5]{2,1,0:T(1,128)S(1)}, s32[1,1,5]{2,1,0:T(1,128)}, u32[]{:S(2)}) copy-start(s32[1,1,5]{2,1,0:T(1,128)} %param.15) | copy-start | bytes 64
  27.3 17.1 %copy-start = (f32[1,2,48,16,256]{4,3,2,1,0:T(8,128)S(1)}, f32[1,2,48,16,256]{4,3,2,1,0:T(8,128)}, u32[]{:S(2)}) copy-start(f32[1,2,48,16,256]{4,3,2,1,0:T(8,128)} %param.9) | copy-start | bytes 4718596
  31.7 15.8 %collective-permute-start.4 = (bf16[3072]{0:T(1024)(128)(2,1)S(1)}, bf16[3072]{0:T(1024)(128)(2,1)S(1)}, u32[]{:S(2)}, u32[]{:S(2)}) collective-permute-start(bf16[3072]{0:T(1024)(128)(2,1)S(1)} %squeeze.24), channel_id=1, source_target_pairs={{0,94},{1,95},{2,0},{3,1},{4,2},{5,3},{6,4},{7,5},{8,6},{9,7},{10,... | collective-permute-start | bytes 18440 | tf_op jit(solution)/shard_map/ppermute | solution.py:27
  34.2 15.3 %collective-permute-start.5 = (bf16[3072]{0:T(1024)(128)(2,1)S(1)}, bf16[3072]{0:T(1024)(128)(2,1)S(1)}, u32[]{:S(2)}, u32[]{:S(2)}) collective-permute-start(bf16[3072]{0:T(1024)(128)(2,1)S(1)} %squeeze.25), channel_id=1, source_target_pairs={{0,95},{1,0},{2,1},{3,2},{4,3},{5,4},{6,5},{7,6},{8,7},{9,8},{10,9... | collective-permute-start | bytes 18440 | tf_op jit(solution)/shard_map/ppermute | solution.py:27
  36.7 12.8 %collective-permute-start.6 = (bf16[3072]{0:T(1024)(128)(2,1)S(1)}, bf16[3072]{0:T(1024)(128)(2,1)S(1)}, u32[]{:S(2)}, u32[]{:S(2)}) collective-permute-start(bf16[3072]{0:T(1024)(128)(2,1)S(1)} %squeeze.26), channel_id=1, source_target_pairs={{0,1},{1,2},{2,3},{3,4},{4,5},{5,6},{6,7},{7,8},{8,9},{9,10},{10,1... | collective-permute-start | bytes 18440 | tf_op jit(solution)/shard_map/ppermute | solution.py:27
  40.1 10.7 %collective-permute-start.7 = (bf16[3072]{0:T(1024)(128)(2,1)S(1)}, bf16[3072]{0:T(1024)(128)(2,1)S(1)}, u32[]{:S(2)}, u32[]{:S(2)}) collective-permute-start(bf16[3072]{0:T(1024)(128)(2,1)S(1)} %squeeze.27), channel_id=1, source_target_pairs={{0,2},{1,3},{2,4},{3,5},{4,6},{5,7},{6,8},{7,9},{8,10},{9,11},{10,... | collective-permute-start | bytes 18440 | tf_op jit(solution)/shard_map/ppermute | solution.py:27
  46.2 6.8 %copy-start.5 = (s32[1,1,5,256]{3,1,2,0:T(1,128)S(1)}, s32[1,1,5,256]{3,1,2,0:T(1,128)}, u32[]{:S(2)}) copy-start(s32[1,1,5,256]{3,1,2,0:T(1,128)} %param.16) | copy-start | bytes 15364
  47.6 29.2 %collective-permute-start.1 = (f32[96,1,256]{2,1,0:T(1,128)}, f32[96,1,256]{2,1,0:T(1,128)S(1)}, u32[]{:S(2)}, u32[]{:S(2)}) collective-permute-start(f32[96,1,256]{2,1,0:T(1,128)} %get-tuple-element.13), channel_id=1, source_target_pairs={{0,1},{1,2},{2,3},{3,4},{4,5},{5,6},{6,7},{7,8},{8,9},{9,10},{10,1... | collective-permute-start | bytes 294920 | tf_op jit(solution)/shard_map/ppermute | solution.py:16
  50.9 10.4 %collective-permute-start.8 = (bf16[5,3072]{1,0:T(8,128)(2,1)S(1)}, bf16[5,3072]{1,0:T(8,128)(2,1)S(1)}, u32[]{:S(2)}, u32[]{:S(2)}) collective-permute-start(bf16[5,3072]{1,0:T(8,128)(2,1)S(1)} %stack.19), channel_id=1, source_target_pairs={{0,384},{96,480},{192,576},{288,672},{384,0},{480,96},{576,192},{6... | collective-permute-start | bytes 92168 | tf_op jit(solution)/shard_map/ppermute | solution.py:31
  73.0 3.7 %copy-start.2 = (f32[1,16,256]{2,1,0:T(8,128)S(1)}, f32[1,16,256]{2,1,0:T(8,128)}, u32[]{:S(2)}) copy-start(f32[1,16,256]{2,1,0:T(8,128)} %param.10) | copy-start | bytes 49156
  80.4 9.1 %collective-permute-start.2 = (f32[96,1,256]{2,1,0:T(1,128)S(1)}, f32[96,1,256]{2,1,0:T(1,128)S(1)}, u32[]{:S(2)}, u32[]{:S(2)}) collective-permute-start(f32[96,1,256]{2,1,0:T(1,128)S(1)} %get-tuple-element.6), channel_id=1, source_target_pairs={{1,0},{2,1},{3,2},{4,3},{5,4},{6,5},{7,6},{8,7},{9,8},{10,9},{11,1... | collective-permute-start | bytes 294920 | tf_op jit(solution)/shard_map/ppermute | solution.py:18
  87.3 10.7 %collective-permute-start.3 = (f32[96,1,256]{2,1,0:T(1,128)S(1)}, f32[96,1,256]{2,1,0:T(1,128)S(1)}, u32[]{:S(2)}, u32[]{:S(2)}) collective-permute-start(f32[96,1,256]{2,1,0:T(1,128)S(1)} %get-tuple-element.7), channel_id=1, source_target_pairs={{0,1},{1,2},{2,3},{3,4},{4,5},{5,6},{6,7},{7,8},{8,9},{9,10},{10,1... | collective-permute-start | bytes 294920 | tf_op jit(solution)/shard_map/ppermute | solution.py:16
where the time goes:
time: 101 us; the launch traced here: 100 us
  starting transfers between devices  42.9 us (42%)
  other arithmetic  20.6 us (20%)
  waiting for transfers between devices  18.2 us (18%)
  local copies, waits for them, and re-layouts  17.8 us (18%)
    ppermute x2, starting transfers between devices, extended(): lax.ppermute(head, axis, [((i + 1) % count, i) for i in range(count)])  24.4 us
    ppermute x4, starting transfers between devices, passed_along(): lax.ppermute(shard, axis, [(i, (i + by) % length) for i in range(length)])  12.6 us
    scatter-add x1, other arithmetic, local(): total.at[dst_index[0, 0].reshape(-1)].add(values.astype(jnp.float32))  10.6 us
    ppermute x2, waiting for transfers between devices, extended(): lax.ppermute(tail, axis, [(i, (i + 1) % count) for i in range(count)])  8.52 us
    ppermute x1, waiting for transfers between devices, partner(): lax.ppermute(shard, axis, [(i, i ^ 1 << distance) for i in range(lax.axis...  8.35 us
    add x2, other arithmetic, advance(): return center + coef[None] * lap  5.33 us
    gather x2, local copies, waits for them, and re-layouts, local(): jnp.take(flux, src_index[0, 0].reshape(-1), axis=1)  4.28 us
    slice x4, local copies, waits for them, and re-layouts, advance(): left = jnp.roll(center, 1, axis=2)  3.93 us
  transfers between devices with their start and end apart: 9, of which 3 were waited for; matrix products, arithmetic and copies ran while one was open for 30% of the time, Pallas kernels for 0%

commit v1 on v0

v1 whole, which is shorter than its diff:
```python
import functools

import jax
import jax.numpy as jnp
from jax import lax
from jax.experimental import pallas as pl
from jax.experimental.pallas import tpu as pltpu
from jax.sharding import PartitionSpec as P

MESH = pl.DeviceIdType.MESH
GROUP = 8
CHUNKS = 4
SLAB = 16


def shift_cols(x, by):
    return pltpu.roll(x, by % x.shape[-1], x.ndim - 1)


def sides(x):
    return shift_cols(x, 1) + shift_cols(x, -1)


def wide(ref, at):
    return jnp.concatenate([ref[0, at, :], ref[1, at, :]], axis=-1)


def put(ref, at, value):
    half = ref.shape[-1]
    ref[0, at, :] = value[:, :half]
    ref[1, at, :] = value[:, half:]


def one_hot(index, count):
    where = lax.broadcasted_iota(jnp.int32, (count, index.shape[1]), 0)
    return jnp.where(where == index, jnp.float32(1.0), jnp.float32(0.0))


def interior_step(low, high, coef, first, last):
    low_up = jnp.where(last, pltpu.roll(high, 7, 1), pltpu.roll(low, 7, 1))
    high_up = jnp.where(last, 0.0, pltpu.roll(high, 7, 1))
    low_down = jnp.where(first, 0.0, pltpu.roll(low, 1, 1))
    high_down = jnp.where(first, pltpu.roll(low, 1, 1), pltpu.roll(high, 1, 1))
    new_low = low + coef[0] * (low_up + low_down + sides(low) - 4.0 * low)
    new_high = high + coef[1] * (high_up + high_down + sides(high) - 4.0 * high)
    return new_low, new_high


def kernel(
    n_comp, n_tile, nvars, nf, entries, slots,
    state, kappa, forcing, gain, src, inter, count, dst, area,
    out, rem,
    field, result, surface, force, coef, cell, src_v, inter_v, dst_v, total,
    edge_out, edge_in, term_out, term_in, spread,
    load_sem, chunk_sem, edge_send, edge_recv, term_send, term_recv, store_sem,
):
    comp, tile = lax.axis_index("comp"), lax.axis_index("tile")
    partner = lax.rem(comp + n_comp // 2, n_comp)
    rows, cols = coef.shape
    levels = field.shape[1] // rows
    lanes = field.shape[2]
    below = (comp, lax.rem(tile + n_tile - 1, n_tile))
    above = (comp, lax.rem(tile + 1, n_tile))
    others = [(partner, lax.rem(tile + n_tile + j - entries // 2, n_tile)) for j in range(entries)]

    barrier = pltpu.get_barrier_semaphore()
    for device in [below, above] + others:
        pl.semaphore_signal(barrier, inc=1, device_id=device, device_id_type=MESH)

    size = field.shape[1] // CHUNKS
    per_var = field.shape[1] // nvars
    loads = [(src, src_v), (inter, inter_v)]
    loads += [(state.at[pl.ds(i * per_var, rows)], surface.at[pl.ds(i * rows, rows)]) for i in range(nvars)]
    loads += [(forcing, force)]
    n_first = len(loads)
    loads += [(kappa, coef), (dst, dst_v), (area, cell)]
    loads = [pltpu.make_async_copy(a, b, load_sem.at[i]) for i, (a, b) in enumerate(loads)]
    chunks = [
        pltpu.make_async_copy(
            state.at[pl.ds(i * size, size), pl.ds(h * lanes, lanes)], field.at[h, pl.ds(i * size, size)], chunk_sem.at[i, h]
        )
        for i in range(CHUNKS)
        for h in range(2)
    ]
    for copy in loads[:n_first] + chunks + loads[n_first:]:
        copy.start()

    for copy in loads[n_first:] + chunks:
        copy.wait()
    for side, (near, far) in enumerate(((0, 1), (rows - 1, rows - 2))):
        edge_out[side, 0:levels, :] = wide(field, pl.ds(near, levels, stride=rows)).astype(jnp.bfloat16)
        edge_out[side, levels:2 * levels, :] = wide(field, pl.ds(far, levels, stride=rows)).astype(jnp.bfloat16)
        edge_out[side, 2 * levels:, :] = jnp.broadcast_to(coef[near:near + 1, :], (16, cols)).astype(jnp.bfloat16)

    pl.semaphore_wait(barrier, 2 + entries)
    edges = [
        pltpu.make_async_remote_copy(
            src_ref=edge_out.at[side], dst_ref=edge_in.at[side], send_sem=edge_send.at[side], recv_sem=edge_recv.at[side],
            device_id=device, device_id_type=MESH,
        )
        for side, device in enumerate((below, above))
    ]
    for copy in edges:
        copy.start()

    for copy in loads[:n_first]:
        copy.wait()
    flux = [
        force[i * rows:(i + 1) * rows, :] + gain[0, i] * surface[(i % nvars) * rows:(i % nvars + 1) * rows, :]
        for i in range(nf)
    ]
    head = [x.astype(jnp.bfloat16) for x in flux]
    tail = [(x - y.astype(jnp.float32)).astype(jnp.bfloat16) for x, y in zip(flux, head, strict=True)]
    both = jnp.concatenate(head + tail, axis=0)
    slot = lax.broadcasted_iota(jnp.int32, (1, slots), 1)
    terms = []
    for j in range(entries):
        index = src_v[j]
        column = one_hot(lax.rem(index, cols), cols).astype(jnp.bfloat16)
        weight = jnp.where(slot < count[0, j], inter_v[j], 0.0)
        pick = one_hot(lax.div(index, cols), rows) * weight
        found = jnp.dot(both, column, preferred_element_type=jnp.float32)
        found = found[:nf * rows] + found[nf * rows:]
        picked = jnp.sum(found.reshape(nf, rows, slots) * pick[None], axis=1)
        term_out[j, :, :] = jnp.concatenate(
            [picked, jnp.zeros((term_out.shape[1] - nf, slots), jnp.float32)], axis=0
        ).astype(jnp.bfloat16)
        copy = pltpu.make_async_remote_copy(
            src_ref=term_out.at[j], dst_ref=term_in.at[j], send_sem=term_send.at[j], recv_sem=term_recv.at[j],
            device_id=others[j], device_id_type=MESH,
        )
        copy.start()
        terms.append(copy)

    row = lax.broadcasted_iota(jnp.int32, (GROUP, 8, cols), 1)
    first, last = row == 0, row == 7
    halves = (coef[0:8, :][None], coef[8:16, :][None])

    def group(i, carry):
        at = pl.multiple_of(i * (GROUP * rows), GROUP * rows)
        block = wide(field, pl.ds(at, GROUP * rows)).reshape(GROUP, rows, cols)
        low, high = block[:, 0:8], block[:, 8:16]
        low, high = interior_step(low, high, halves, first, last)
        low, high = interior_step(low, high, halves, first, last)
        put(result, pl.ds(at, GROUP * rows), jnp.concatenate([low, high], axis=1).reshape(GROUP * rows, cols))
        return carry

    lax.fori_loop(0, levels // GROUP, group, 0)

    for j in range(entries):
        spread[:, j * slots:(j + 1) * slots] = one_hot(lax.rem(dst_v[j], cols), cols).astype(jnp.bfloat16)
    inverse = 1.0 / cell[...]

    acc = jnp.zeros((nf * rows, cols), jnp.float32)
    for j in range(entries):
        terms[j].wait()
        here = one_hot(lax.div(dst_v[j], cols), rows)
        value = term_in[j].astype(jnp.float32)
        placed = jnp.concatenate([value[i:i + 1, :] * here for i in range(nf)], axis=0).astype(jnp.bfloat16)
        acc = acc + lax.dot_general(
            placed, spread[:, j * slots:(j + 1) * slots], (((1,), (1,)), ((), ())), preferred_element_type=jnp.float32
        )
    for i in range(nf):
        total[i * rows:(i + 1) * rows, :] = acc[i * rows:(i + 1) * rows, :] * inverse
    stores = [pltpu.make_async_copy(total, rem, store_sem.at[0])]
    stores[0].start()

    for copy in edges:
        copy.wait()
    for side, (near, far) in ((1, (0, 1)), (0, (rows - 1, rows - 2))):
        k_near, k_far = coef[near:near + 1, :], coef[far:far + 1, :]
        k_out = edge_in[side, 2 * levels:, :].astype(jnp.float32)[0:1, :]
        for g in range(0, levels, SLAB):
            h = edge_in[side, g:g + SLAB, :].astype(jnp.float32)
            h2 = edge_in[side, levels + g:levels + g + SLAB, :].astype(jnp.float32)
            at_near = pl.ds(near + g * rows, SLAB, stride=rows)
            at_far = pl.ds(far + g * rows, SLAB, stride=rows)
            a = h + k_out * (h2 + sides(h) - 4.0 * h + wide(field, at_near))
            b = k_near * h
            put(result, at_near, wide(result, at_near) + (b + k_near * (a + sides(b) - 4.0 * b)))
            put(result, at_far, wide(result, at_far) + k_far * b)
    for h in range(2):
        copy = pltpu.make_async_copy(result.at[h], out.at[:, pl.ds(h * lanes, lanes)], store_sem.at[1 + h])
        copy.start()
        stores.append(copy)
    for copy in stores:
        copy.wait()


def local(state, kappa, forcing, flux_gain, src_index, intersection, pair_count, dst_index, cell_area):
    _, nvars, deep, rows, cols = state.shape
    nf = forcing.shape[1]
    entries, slots = src_index.shape[2:]
    levels = nvars * deep
    n_comp, n_tile = lax.axis_size("comp"), lax.axis_size("tile")
    hbm = pl.BlockSpec(memory_space=pl.ANY)
    smem = pl.BlockSpec(memory_space=pltpu.SMEM)
    pad = -(-nf // 16) * 16
    f32, bf16, i32 = jnp.float32, jnp.bfloat16, jnp.int32
    dma = pltpu.SemaphoreType.DMA
    n_loads = nvars + 6
    out, rem = pl.pallas_call(
        functools.partial(kernel, n_comp, n_tile, nvars, nf, entries, slots),
        out_shape=(
            jax.ShapeDtypeStruct((levels * rows, cols), f32),
            jax.ShapeDtypeStruct((nf * rows, cols), f32),
        ),
        in_specs=[hbm, hbm, hbm, smem, hbm, hbm, smem, hbm, hbm],
        out_specs=(hbm, hbm),
        scratch_shapes=[
            pltpu.VMEM((2, levels * rows, cols // 2), f32),
            pltpu.VMEM((2, levels * rows, cols // 2), f32),
            pltpu.VMEM((nvars * rows, cols), f32),
            pltpu.VMEM((nf * rows, cols), f32),
            pltpu.VMEM((rows, cols), f32),
            pltpu.VMEM((rows, cols), f32),
            pltpu.VMEM((entries, 1, slots), i32),
            pltpu.VMEM((entries, 1, slots), f32),
            pltpu.VMEM((entries, 1, slots), i32),
            pltpu.VMEM((nf * rows, cols), f32),
            pltpu.VMEM((2, 2 * levels + 16, cols), bf16),
            pltpu.VMEM((2, 2 * levels + 16, cols), bf16),
            pltpu.VMEM((entries, pad, slots), bf16),
            pltpu.VMEM((entries, pad, slots), bf16),
            pltpu.VMEM((cols, entries * slots), bf16),
            dma((n_loads,)),
            dma((CHUNKS, 2)),
            dma((2,)),
            dma((2,)),
            dma((entries,)),
            dma((entries,)),
            dma((3,)),
        ],
        compiler_params=pltpu.CompilerParams(
            collective_id=0, has_side_effects=True, vmem_limit_bytes=56 * 1024 * 1024
        ),
        cost_estimate=pl.CostEstimate(flops=10**8, bytes_accessed=4 * 10**6, transcendentals=0),
    )(
        state.reshape(levels * rows, cols),
        kappa[0],
        forcing.reshape(nf * rows, cols),
        flux_gain,
        src_index.reshape(entries, 1, slots),
        intersection.reshape(entries, 1, slots),
        pair_count.reshape(1, entries),
        dst_index.reshape(entries, 1, slots),
        cell_area[0],
    )
    return out.reshape(1, nvars, deep, rows, cols), rem.reshape(1, nf, rows, cols)


def solution(mesh):
    return jax.shard_map(
        local,
        mesh=mesh,
        in_specs=(
            P("comp", None, None, "tile", None),
            P("comp", "tile", None),
            P("comp", None, "tile", None),
            P("comp", None),
            P("comp", "tile", None, None),
            P("comp", "tile", None, None),
            P("comp", "tile", None),
            P("comp", "tile", None, None),
            P("comp", "tile", None),
        ),
        out_specs=(P("comp", None, None, "tile", None), P("comp", None, "tile", None)),
        check_vma=False,
    )
```

time: 101 us -> 32.7 us (0.32)
  the two profiles are of different devices: /device:TPU:40 before, /device:TPU:1 now
where the time goes in v1:
time: 32.7 us; the launch traced here: 32.5 us
  Pallas kernels  28.5 us (87%)
  local copies, waits for them, and re-layouts  3.39 us (10%)
  between operations  0.65 us (2%)
    pallas_call x1, Pallas kernels, local(): pl.pallas_call(functools.partial(kernel, n_comp, n_tile, nvars, nf, entri...  28.5 us
    unnamed x4, local copies, waits for them, and re-layouts  3.39 us

profile of v1, /device:TPU:1, one launch (start us, length us, event | category | flops | bytes accessed | tf_op | source)
XLA Modules:
  0.0 32.5 jit_solution(7607599705516757398)
XLA Ops:
  0.6 28.5 %shard_map.104 = (f32[1536,256]{1,0:T(8,128)}, f32[192,256]{1,0:T(8,128)}) custom-call(f32[1536,256]{1,0:T(8,128)} %bitcast.10, f32[16,256]{1,0:T(8,128)} %bitcast.14, f32[192,256]{1,0:T(8,128)} %bitcast.12, f32[1,12]{1,0:T(1,128)} %gain.1, s32[5,1,256]{2,1,0:T(1,128)} %bitcast.16, f32[5,1,256]{2,1,0:T(1,128)} %bitcast.17, s32[1,5]{1,0:T(1,128)} %bitcast.19, ...), custom_call_target="tpu_custom_call" | custom-call | flops 100000000 | bytes 4000000 | tf_op jit(solution)/shard_map/pallas_call | solution.py:202
  29.1 0.0 copy-start
  29.2 2.7 %copy.13 = f32[1,2,48,16,256]{4,3,2,1,0:T(8,128)} copy(f32[1,2,48,16,256]{4,3,2,1,0:T(8,128)} %bitcast.11) | data formatting | bytes 3145728
  31.9 0.0 copy-done
  31.9 0.7 %copy.14 = f32[1,12,16,256]{3,2,1,0:T(8,128)} copy(f32[1,12,16,256]{3,2,1,0:T(8,128)S(1)} %bitcast.13) | data formatting | bytes 393216
Async XLA Ops:
  29.1 2.7 %copy-start = (f32[192,256]{1,0:T(8,128)S(1)}, f32[192,256]{1,0:T(8,128)}, u32[]{:S(2)}) copy-start(f32[192,256]{1,0:T(8,128)} %get-tuple-element.5) | copy-start | bytes 589828

commit v2 on v1

--- a/solution.py
+++ b/solution.py
@@ -11,6 +11,7 @@
 GROUP = 8
 CHUNKS = 4
 SLAB = 16
+LIMIT = 40 * 1024 * 1024
 
 
 def shift_cols(x, by):
@@ -49,10 +50,10 @@
 def kernel(
     n_comp, n_tile, nvars, nf, entries, slots,
     state, kappa, forcing, gain, src, inter, count, dst, area,
-    out, rem,
-    field, result, surface, force, coef, cell, src_v, inter_v, dst_v, total,
-    edge_out, edge_in, term_out, term_in, spread,
-    load_sem, chunk_sem, edge_send, edge_recv, term_send, term_recv, store_sem,
+    result, term_in, spread, masks, inverse,
+    field, surface, force, coef, cell, src_v, inter_v, dst_v,
+    edge_out, edge_in, term_out,
+    load_sem, chunk_sem, edge_send, edge_recv, term_send, term_recv,
 ):
     comp, tile = lax.axis_index("comp"), lax.axis_index("tile")
     partner = lax.rem(comp + n_comp // 2, n_comp)
@@ -148,22 +149,9 @@
     lax.fori_loop(0, levels // GROUP, group, 0)
 
     for j in range(entries):
-        spread[:, j * slots:(j + 1) * slots] = one_hot(lax.rem(dst_v[j], cols), cols).astype(jnp.bfloat16)
-    inverse = 1.0 / cell[...]
-
-    acc = jnp.zeros((nf * rows, cols), jnp.float32)
-    for j in range(entries):
-        terms[j].wait()
-        here = one_hot(lax.div(dst_v[j], cols), rows)
-        value = term_in[j].astype(jnp.float32)
-        placed = jnp.concatenate([value[i:i + 1, :] * here for i in range(nf)], axis=0).astype(jnp.bfloat16)
-        acc = acc + lax.dot_general(
-            placed, spread[:, j * slots:(j + 1) * slots], (((1,), (1,)), ((), ())), preferred_element_type=jnp.float32
-        )
-    for i in range(nf):
-        total[i * rows:(i + 1) * rows, :] = acc[i * rows:(i + 1) * rows, :] * inverse
-    stores = [pltpu.make_async_copy(total, rem, store_sem.at[0])]
-    stores[0].start()
+        spread[j * slots:(j + 1) * slots, :] = one_hot(lax.rem(dst_v[j], cols), cols).T.astype(jnp.bfloat16)
+        masks[j, :, :] = one_hot(lax.div(dst_v[j], cols), rows)
+    inverse[...] = 1.0 / cell[...]
 
     for copy in edges:
         copy.wait()
@@ -179,10 +167,29 @@
             b = k_near * h
             put(result, at_near, wide(result, at_near) + (b + k_near * (a + sides(b) - 4.0 * b)))
             put(result, at_far, wide(result, at_far) + k_far * b)
-    for h in range(2):
-        copy = pltpu.make_async_copy(result.at[h], out.at[:, pl.ds(h * lanes, lanes)], store_sem.at[1 + h])
-        copy.start()
-        stores.append(copy)
+    for copy in terms:
+        copy.wait()
+
+
+def finish_kernel(nvars, nf, entries, slots, result, term_in, spread, masks, inverse, out, rem, total, store_sem):
+    lanes = result.shape[2]
+    rows, cols = inverse.shape
+    stores = [
+        pltpu.make_async_copy(result.at[h], out.at[:, pl.ds(h * lanes, lanes)], store_sem.at[h]) for h in range(2)
+    ]
+    for copy in stores:
+        copy.start()
+    placed = []
+    for j in range(entries):
+        value = term_in[j].astype(jnp.float32)
+        here = masks[j]
+        placed.append(jnp.concatenate([value[i:i + 1, :] * here for i in range(nf)], axis=0).astype(jnp.bfloat16))
+    acc = jnp.dot(jnp.concatenate(placed, axis=1), spread[...], preferred_element_type=jnp.float32)
+    scale = inverse[...]
+    for i in range(nf):
+        total[i * rows:(i + 1) * rows, :] = acc[i * rows:(i + 1) * rows, :] * scale
+    stores.append(pltpu.make_async_copy(total, rem, store_sem.at[2]))
+    stores[-1].start()
     for copy in stores:
         copy.wait()
 
@@ -199,16 +206,19 @@
     f32, bf16, i32 = jnp.float32, jnp.bfloat16, jnp.int32
     dma = pltpu.SemaphoreType.DMA
     n_loads = nvars + 6
-    out, rem = pl.pallas_call(
+    vmem = pl.BlockSpec(memory_space=pltpu.VMEM)
+    passed = pl.pallas_call(
         functools.partial(kernel, n_comp, n_tile, nvars, nf, entries, slots),
         out_shape=(
-            jax.ShapeDtypeStruct((levels * rows, cols), f32),
-            jax.ShapeDtypeStruct((nf * rows, cols), f32),
+            pltpu.VMEM((2, levels * rows, cols // 2), f32),
+            pltpu.VMEM((entries, pad, slots), bf16),
+            pltpu.VMEM((entries * slots, cols), bf16),
+            pltpu.VMEM((entries, rows, slots), f32),
+            pltpu.VMEM((rows, cols), f32),
         ),
         in_specs=[hbm, hbm, hbm, smem, hbm, hbm, smem, hbm, hbm],
-        out_specs=(hbm, hbm),
+        out_specs=(vmem,) * 5,
         scratch_shapes=[
-            pltpu.VMEM((2, levels * rows, cols // 2), f32),
             pltpu.VMEM((2, levels * rows, cols // 2), f32),
             pltpu.VMEM((nvars * rows, cols), f32),
             pltpu.VMEM((nf * rows, cols), f32),
@@ -217,35 +227,48 @@
             pltpu.VMEM((entries, 1, slots), i32),
             pltpu.VMEM((entries, 1, slots), f32),
             pltpu.VMEM((entries, 1, slots), i32),
-            pltpu.VMEM((nf * rows, cols), f32),
             pltpu.VMEM((2, 2 * levels + 16, cols), bf16),
             pltpu.VMEM((2, 2 * levels + 16, cols), bf16),
             pltpu.VMEM((entries, pad, slots), bf16),
-            pltpu.VMEM((entries, pad, slots), bf16),
-            pltpu.VMEM((cols, entries * slots), bf16),
             dma((n_loads,)),
             dma((CHUNKS, 2)),
             dma((2,)),
             dma((2,)),
             dma((entries,)),
             dma((entries,)),
-            dma((3,)),
         ],
         compiler_params=pltpu.CompilerParams(
-            collective_id=0, has_side_effects=True, vmem_limit_bytes=56 * 1024 * 1024
+            collective_id=0, has_side_effects=True, vmem_limit_bytes=LIMIT
         ),
         cost_estimate=pl.CostEstimate(flops=10**8, bytes_accessed=4 * 10**6, transcendentals=0),
     )(
-        state.reshape(levels * rows, cols),
-        kappa[0],
-        forcing.reshape(nf * rows, cols),
-        flux_gain,
-        src_index.reshape(entries, 1, slots),
-        intersection.reshape(entries, 1, slots),
-        pair_count.reshape(1, entries),
-        dst_index.reshape(entries, 1, slots),
-        cell_area[0],
+        *[
+            pltpu.with_memory_space_constraint(x, pltpu.HBM)
+            for x in (
+                state.reshape(levels * rows, cols),
+                kappa[0],
+                forcing.reshape(nf * rows, cols),
+                flux_gain,
+                src_index.reshape(entries, 1, slots),
+                intersection.reshape(entries, 1, slots),
+                pair_count.reshape(1, entries),
+                dst_index.reshape(entries, 1, slots),
+                cell_area[0],
+            )
+        ]
     )
+    out, rem = pl.pallas_call(
+        functools.partial(finish_kernel, nvars, nf, entries, slots),
+        out_shape=(
+            jax.ShapeDtypeStruct((levels * rows, cols), f32),
+            jax.ShapeDtypeStruct((nf * rows, cols), f32),
+        ),
+        in_specs=[vmem] * 5,
+        out_specs=(hbm, hbm),
+        scratch_shapes=[pltpu.VMEM((nf * rows, cols), f32), dma((3,))],
+        compiler_params=pltpu.CompilerParams(vmem_limit_bytes=LIMIT),
+        cost_estimate=pl.CostEstimate(flops=10**8, bytes_accessed=4 * 10**6, transcendentals=0),
+    )(*passed)
     return out.reshape(1, nvars, deep, rows, cols), rem.reshape(1, nf, rows, cols)
 
 

time: 32.7 us -> 28.7 us (0.88)
  local copies, waits for them, and re-layouts: 3.39 us -> 0 us
  Pallas kernels: 28.5 us -> 27.9 us
    unnamed x4 -> x0, local copies, waits for them, and re-layouts: 3.39 us -> none
    pallas_call x1, Pallas kernels: 28.5 us -> 26.7 us  [local(): pl.pallas_call(functools.partial(kernel, n_comp, n_tile, nvars, nf, entri...]
    pallas_call x0 -> x1, Pallas kernels: none -> 1.24 us  [local(): pl.pallas_call(functools.partial(finish_kernel, nvars, nf, entries, slots...]
where the time goes in v2:
time: 28.7 us; the launch traced here: 28.5 us
  Pallas kernels  27.9 us (97%)
  between operations  0.64 us (2%)
    pallas_call x1, Pallas kernels, local(): pl.pallas_call(functools.partial(kernel, n_comp, n_tile, nvars, nf, entri...  26.7 us
    pallas_call x1, Pallas kernels, local(): pl.pallas_call(functools.partial(finish_kernel, nvars, nf, entries, slots...  1.24 us

profile of v2, /device:TPU:1, one launch (start us, length us, event | category | flops | bytes accessed | tf_op | source)
XLA Modules:
  0.0 28.5 jit_solution(17341438455191253614)
XLA Ops:
  0.6 26.7 %shard_map.104 = (f32[2,1536,128]{2,1,0:T(8,128)S(1)}, bf16[5,16,256]{2,1,0:T(8,128)(2,1)S(1)}, bf16[1280,256]{1,0:T(8,128)(2,1)S(1)}, f32[5,16,256]{2,1,0:T(8,128)S(1)}, f32[16,256]{1,0:T(8,128)S(1)}) custom-call(f32[1536,256]{1,0:T(8,128)} %bitcast.10, f32[16,256]{1,0:T(8,128)} %bitcast.12, f32[192,256]{1,0:T(8,128)} %bitcast.11, f32[1,12]{1,0:T(1,128)} %gain.1, ...), custom_call_target="tpu_custom_call" | custom-call | flops 100000000 | bytes 4000000 | tf_op jit(solution)/shard_map/pallas_call | solution.py:210
  27.3 1.2 %shard_map.105 = (f32[1536,256]{1,0:T(8,128)}, f32[192,256]{1,0:T(8,128)}) custom-call(f32[2,1536,128]{2,1,0:T(8,128)S(1)} %get-tuple-element.9.result, bf16[5,16,256]{2,1,0:T(8,128)(2,1)S(1)} %get-tuple-element.10.term_in, bf16[1280,256]{1,0:T(8,128)(2,1)S(1)} %get-tuple-element.11.spread, f32[5,16,256]{2,1,0:T(8,128)S(1)} %get-tuple-element.12.masks, ...), custom_call_target="tpu_custom_call" | custom-call | flops 100000000 | bytes 4000000 | tf_op jit(solution)/shard_map/pallas_call | solution.py:260

commit v3 on v2

--- a/solution.py
+++ b/solution.py
@@ -11,6 +11,7 @@
 GROUP = 8
 CHUNKS = 4
 SLAB = 16
+DEPTH = 12
 LIMIT = 40 * 1024 * 1024
 
 
@@ -51,87 +52,148 @@
     n_comp, n_tile, nvars, nf, entries, slots,
     state, kappa, forcing, gain, src, inter, count, dst, area,
     result, term_in, spread, masks, inverse,
-    field, surface, force, coef, cell, src_v, inter_v, dst_v,
+    field, surface, force, coef, cell, src_v, inter_v, dst_v, gain_s, count_s,
     edge_out, edge_in, term_out,
-    load_sem, chunk_sem, edge_send, edge_recv, term_send, term_recv,
+    ready, load_sem, edge_send, edge_recv, term_send, term_recv,
 ):
     comp, tile = lax.axis_index("comp"), lax.axis_index("tile")
     partner = lax.rem(comp + n_comp // 2, n_comp)
     rows, cols = coef.shape
     levels = field.shape[1] // rows
     lanes = field.shape[2]
+    shift = cols.bit_length() - 1
     below = (comp, lax.rem(tile + n_tile - 1, n_tile))
     above = (comp, lax.rem(tile + 1, n_tile))
     others = [(partner, lax.rem(tile + n_tile + j - entries // 2, n_tile)) for j in range(entries)]
 
+    half = n_tile // 2
+    deep = min(DEPTH, half)
+    wide_by = half // deep
+    x, z, y = lax.rem(lax.div(tile, deep), wide_by), lax.rem(tile, deep), 2 * lax.div(comp, 2) + lax.div(tile, half)
+
+    def rank(offset, across):
+        over, under = z + offset >= deep, z + offset < 0
+        z_there = z + offset + jnp.where(under, deep, 0) - jnp.where(over, deep, 0)
+        x_there = x + jnp.where(over, 1, 0) - jnp.where(under, 1, 0)
+        turn = jnp.logical_or(x_there == wide_by, x_there < 0)
+        x_there = jnp.where(turn, jnp.where(over, 0, wide_by - 1), x_there)
+        y_there = jnp.where(turn, y + 1 - 2 * lax.rem(y, 2), y)
+        if across:
+            y_there = lax.rem(y_there + n_comp // 2, n_comp)
+        when = 13 * jnp.minimum(z_there, 7) + 4 * jnp.maximum(z_there - 7, 0) + 4 * x_there
+        when = when + jnp.where(y_there < 4, 6 * y_there, 42 - 3 * y_there)
+        to_tile = lax.rem(tile + n_tile + offset, n_tile)
+        return (when * n_comp + (partner if across else comp)) * n_tile + to_tile
+
+    own = rank(0, False)
+
+    def after(offset, across):
+        return rank(offset, across) > own
+
+    peers = {}
+    for j in range(entries):
+        offset = j - entries // 2
+        peers["term", offset] = (others[j], after(offset, True), j, entries - 1 - j, j)
+    peers["edge", -1] = (below, after(-1, False), 0, 1, entries)
+    peers["edge", 1] = (above, after(1, False), 1, 0, entries + 1)
+    order = [("term", 0), ("edge", 1), ("term", 1), ("term", 2), ("edge", -1), ("term", -2), ("term", -1)]
+
+    sends = [("term", 1), ("term", 2), ("term", -2), ("term", -1), ("term", 0), ("edge", 1), ("edge", -1)]
     barrier = pltpu.get_barrier_semaphore()
-    for device in [below, above] + others:
-        pl.semaphore_signal(barrier, inc=1, device_id=device, device_id_type=MESH)
+    before = 0
+    for key in order:
+        device, is_after = peers[key][:2]
+
+        @pl.when(is_after)
+        def _(device=device):
+            pl.semaphore_signal(barrier, inc=1, device_id=device, device_id_type=MESH)
+
+        before = before + jnp.where(is_after, 0, 1)
 
     size = field.shape[1] // CHUNKS
     per_var = field.shape[1] // nvars
-    loads = [(src, src_v), (inter, inter_v)]
-    loads += [(state.at[pl.ds(i * per_var, rows)], surface.at[pl.ds(i * rows, rows)]) for i in range(nvars)]
-    loads += [(forcing, force)]
-    n_first = len(loads)
-    loads += [(kappa, coef), (dst, dst_v), (area, cell)]
-    loads = [pltpu.make_async_copy(a, b, load_sem.at[i]) for i, (a, b) in enumerate(loads)]
-    chunks = [
-        pltpu.make_async_copy(
-            state.at[pl.ds(i * size, size), pl.ds(h * lanes, lanes)], field.at[h, pl.ds(i * size, size)], chunk_sem.at[i, h]
-        )
+    early = [(src, src_v), (gain, gain_s), (count, count_s), (inter, inter_v)]
+    early += [(state.at[pl.ds(i * per_var, rows)], surface.at[pl.ds(i * rows, rows)]) for i in range(nvars)]
+    early += [(forcing, force)]
+    middle = [(kappa, coef)] + [
+        (state.at[pl.ds(i * size, size), pl.ds(h * lanes, lanes)], field.at[h, pl.ds(i * size, size)])
         for i in range(CHUNKS)
         for h in range(2)
     ]
-    for copy in loads[:n_first] + chunks + loads[n_first:]:
+    late = [(dst, dst_v), (area, cell)]
+    copies = [pltpu.make_async_copy(a, b, load_sem.at[i]) for i, (a, b) in enumerate(early + middle + late)]
+    early, middle, late = copies[:len(early)], copies[len(early):len(early) + len(middle)], copies[-len(late):]
+    for copy in copies:
         copy.start()
 
-    for copy in loads[n_first:] + chunks:
+    @pl.when(before > 0)
+    def _():
+        pl.semaphore_wait(barrier, before)
+
+    for key in sends:
+        device, is_after, _, _, number = peers[key]
+
+        @pl.when(jnp.logical_not(is_after))
+        def _(device=device, number=number):
+            pl.semaphore_signal(ready.at[number], inc=1, device_id=device, device_id_type=MESH)
+
+    for copy in early:
+        copy.wait()
+    flux = [
+        force[i * rows:(i + 1) * rows, :] + gain_s[0, i] * surface[(i % nvars) * rows:(i % nvars + 1) * rows, :]
+        for i in range(nf)
+    ]
+    head = [x.astype(jnp.bfloat16) for x in flux]
+    tail = [(x - y.astype(jnp.float32)).astype(jnp.bfloat16) for x, y in zip(flux, head, strict=True)]
+    both = jnp.concatenate([jnp.concatenate(head, axis=0), jnp.concatenate(tail, axis=0)], axis=1)
+    slot = lax.broadcasted_iota(jnp.int32, (1, slots), 1)
+    for j in range(entries):
+        index = src_v[j]
+        column = one_hot(index & (cols - 1), cols).astype(jnp.bfloat16)
+        weight = jnp.where(slot < count_s[0, j], inter_v[j], 0.0)
+        pick = one_hot(index >> shift, rows) * weight
+        found = jnp.dot(both, jnp.concatenate([column, column], axis=0), preferred_element_type=jnp.float32)
+        picked = jnp.sum(found.reshape(nf, rows, slots) * pick[None], axis=1)
+        term_out[j, :, :] = jnp.concatenate(
+            [picked, jnp.zeros((term_out.shape[1] - nf, slots), jnp.float32)], axis=0
+        ).astype(jnp.bfloat16)
+
+    def to(key):
+        device, _, out_slot = peers[key][:3]
+        here, there, done, came = (
+            (term_out, term_in, term_send, term_recv) if key[0] == "term" else (edge_out, edge_in, edge_send, edge_recv)
+        )
+        return pltpu.make_async_remote_copy(
+            src_ref=here.at[out_slot], dst_ref=there.at[out_slot], send_sem=done.at[out_slot], recv_sem=came.at[out_slot],
+            device_id=device, device_id_type=MESH,
+        )
+
+    def arrived(key):
+        slot_in = peers[key][3]
+        there, done, came = (term_in, term_send, term_recv) if key[0] == "term" else (edge_in, edge_send, edge_recv)
+        pltpu.make_async_remote_copy(
+            src_ref=there.at[slot_in], dst_ref=there.at[slot_in], send_sem=done.at[slot_in], recv_sem=came.at[slot_in],
+            device_id=peers[key][0], device_id_type=MESH,
+        ).wait_recv()
+
+    for key in sends[:entries]:
+
+        @pl.when(jnp.logical_not(peers[key][1]))
+        def _(key=key):
+            to(key).start()
+
+    for copy in middle:
         copy.wait()
     for side, (near, far) in enumerate(((0, 1), (rows - 1, rows - 2))):
         edge_out[side, 0:levels, :] = wide(field, pl.ds(near, levels, stride=rows)).astype(jnp.bfloat16)
         edge_out[side, levels:2 * levels, :] = wide(field, pl.ds(far, levels, stride=rows)).astype(jnp.bfloat16)
         edge_out[side, 2 * levels:, :] = jnp.broadcast_to(coef[near:near + 1, :], (16, cols)).astype(jnp.bfloat16)
 
-    pl.semaphore_wait(barrier, 2 + entries)
-    edges = [
-        pltpu.make_async_remote_copy(
-            src_ref=edge_out.at[side], dst_ref=edge_in.at[side], send_sem=edge_send.at[side], recv_sem=edge_recv.at[side],
-            device_id=device, device_id_type=MESH,
-        )
-        for side, device in enumerate((below, above))
-    ]
-    for copy in edges:
-        copy.start()
-
-    for copy in loads[:n_first]:
-        copy.wait()
-    flux = [
-        force[i * rows:(i + 1) * rows, :] + gain[0, i] * surface[(i % nvars) * rows:(i % nvars + 1) * rows, :]
-        for i in range(nf)
-    ]
-    head = [x.astype(jnp.bfloat16) for x in flux]
-    tail = [(x - y.astype(jnp.float32)).astype(jnp.bfloat16) for x, y in zip(flux, head, strict=True)]
-    both = jnp.concatenate(head + tail, axis=0)
-    slot = lax.broadcasted_iota(jnp.int32, (1, slots), 1)
-    terms = []
-    for j in range(entries):
-        index = src_v[j]
-        column = one_hot(lax.rem(index, cols), cols).astype(jnp.bfloat16)
-        weight = jnp.where(slot < count[0, j], inter_v[j], 0.0)
-        pick = one_hot(lax.div(index, cols), rows) * weight
-        found = jnp.dot(both, column, preferred_element_type=jnp.float32)
-        found = found[:nf * rows] + found[nf * rows:]
-        picked = jnp.sum(found.reshape(nf, rows, slots) * pick[None], axis=1)
-        term_out[j, :, :] = jnp.concatenate(
-            [picked, jnp.zeros((term_out.shape[1] - nf, slots), jnp.float32)], axis=0
-        ).astype(jnp.bfloat16)
-        copy = pltpu.make_async_remote_copy(
-            src_ref=term_out.at[j], dst_ref=term_in.at[j], send_sem=term_send.at[j], recv_sem=term_recv.at[j],
-            device_id=others[j], device_id_type=MESH,
-        )
-        copy.start()
-        terms.append(copy)
+    for key in sends[entries:]:
+
+        @pl.when(jnp.logical_not(peers[key][1]))
+        def _(key=key):
+            to(key).start()
 
     row = lax.broadcasted_iota(jnp.int32, (GROUP, 8, cols), 1)
     first, last = row == 0, row == 7
@@ -148,13 +210,23 @@
 
     lax.fori_loop(0, levels // GROUP, group, 0)
 
+    for copy in late:
+        copy.wait()
     for j in range(entries):
-        spread[j * slots:(j + 1) * slots, :] = one_hot(lax.rem(dst_v[j], cols), cols).T.astype(jnp.bfloat16)
-        masks[j, :, :] = one_hot(lax.div(dst_v[j], cols), rows)
+        spread[j * slots:(j + 1) * slots, :] = one_hot(dst_v[j] & (cols - 1), cols).T.astype(jnp.bfloat16)
+        masks[j, :, :] = one_hot(dst_v[j] >> shift, rows)
     inverse[...] = 1.0 / cell[...]
 
-    for copy in edges:
-        copy.wait()
+    for key in order:
+
+        @pl.when(peers[key][1])
+        def _(key=key):
+            kind, offset = key
+            pl.semaphore_wait(ready.at[peers[kind, -offset][4]], 1)
+            to(key).start()
+
+    arrived(("edge", 1))
+    arrived(("edge", -1))
     for side, (near, far) in ((1, (0, 1)), (0, (rows - 1, rows - 2))):
         k_near, k_far = coef[near:near + 1, :], coef[far:far + 1, :]
         k_out = edge_in[side, 2 * levels:, :].astype(jnp.float32)[0:1, :]
@@ -167,8 +239,11 @@
             b = k_near * h
             put(result, at_near, wide(result, at_near) + (b + k_near * (a + sides(b) - 4.0 * b)))
             put(result, at_far, wide(result, at_far) + k_far * b)
-    for copy in terms:
-        copy.wait()
+    for key in order:
+        if key[0] == "term":
+            arrived(key)
+    for key in order:
+        to(key).wait_send()
 
 
 def finish_kernel(nvars, nf, entries, slots, result, term_in, spread, masks, inverse, out, rem, total, store_sem):
@@ -201,11 +276,10 @@
     levels = nvars * deep
     n_comp, n_tile = lax.axis_size("comp"), lax.axis_size("tile")
     hbm = pl.BlockSpec(memory_space=pl.ANY)
-    smem = pl.BlockSpec(memory_space=pltpu.SMEM)
     pad = -(-nf // 16) * 16
     f32, bf16, i32 = jnp.float32, jnp.bfloat16, jnp.int32
     dma = pltpu.SemaphoreType.DMA
-    n_loads = nvars + 6
+    n_loads = nvars + 8 + 2 * CHUNKS
     vmem = pl.BlockSpec(memory_space=pltpu.VMEM)
     passed = pl.pallas_call(
         functools.partial(kernel, n_comp, n_tile, nvars, nf, entries, slots),
@@ -216,7 +290,7 @@
             pltpu.VMEM((entries, rows, slots), f32),
             pltpu.VMEM((rows, cols), f32),
         ),
-        in_specs=[hbm, hbm, hbm, smem, hbm, hbm, smem, hbm, hbm],
+        in_specs=[hbm] * 9,
         out_specs=(vmem,) * 5,
         scratch_shapes=[
             pltpu.VMEM((2, levels * rows, cols // 2), f32),
@@ -227,11 +301,13 @@
             pltpu.VMEM((entries, 1, slots), i32),
             pltpu.VMEM((entries, 1, slots), f32),
             pltpu.VMEM((entries, 1, slots), i32),
+            pltpu.SMEM((1, nf), f32),
+            pltpu.SMEM((1, entries), i32),
             pltpu.VMEM((2, 2 * levels + 16, cols), bf16),
             pltpu.VMEM((2, 2 * levels + 16, cols), bf16),
             pltpu.VMEM((entries, pad, slots), bf16),
+            pltpu.SemaphoreType.REGULAR((entries + 2,)),
             dma((n_loads,)),
-            dma((CHUNKS, 2)),
             dma((2,)),
             dma((2,)),
             dma((entries,)),

time: 28.7 us -> 26.8 us (0.934)
  Pallas kernels: 27.9 us -> 25.9 us
    pallas_call x1, Pallas kernels: 26.7 us -> 24.7 us  [local(): pl.pallas_call(functools.partial(kernel, n_comp, n_tile, nvars, nf, entri...]
where the time goes in v3:
time: 26.8 us; the launch traced here: 26.5 us
  Pallas kernels  25.9 us (97%)
  between operations  0.64 us (2%)
    pallas_call x1, Pallas kernels, local(): pl.pallas_call(functools.partial(kernel, n_comp, n_tile, nvars, nf, entri...  24.7 us
    pallas_call x1, Pallas kernels, local(): pl.pallas_call(functools.partial(finish_kernel, nvars, nf, entries, slots...  1.24 us

profile of v3, /device:TPU:1, one launch (start us, length us, event | category | flops | bytes accessed | tf_op | source)
XLA Modules:
  0.0 26.5 jit_solution(8283650603336043177)
XLA Ops:
  0.6 24.7 %shard_map.104 = (f32[2,1536,128]{2,1,0:T(8,128)S(1)}, bf16[5,16,256]{2,1,0:T(8,128)(2,1)S(1)}, bf16[1280,256]{1,0:T(8,128)(2,1)S(1)}, f32[5,16,256]{2,1,0:T(8,128)S(1)}, f32[16,256]{1,0:T(8,128)S(1)}) custom-call(f32[1536,256]{1,0:T(8,128)} %bitcast.10, f32[16,256]{1,0:T(8,128)} %bitcast.12, f32[192,256]{1,0:T(8,128)} %bitcast.11, f32[1,12]{1,0:T(1,128)} %gain.1, ...), custom_call_target="tpu_custom_call" | custom-call | flops 100000000 | bytes 4000000 | tf_op jit(solution)/shard_map/pallas_call | solution.py:284
  25.3 1.2 %shard_map.105 = (f32[1536,256]{1,0:T(8,128)}, f32[192,256]{1,0:T(8,128)}) custom-call(f32[2,1536,128]{2,1,0:T(8,128)S(1)} %get-tuple-element.9.result, bf16[5,16,256]{2,1,0:T(8,128)(2,1)S(1)} %get-tuple-element.10.term_in, bf16[1280,256]{1,0:T(8,128)(2,1)S(1)} %get-tuple-element.11.spread, f32[5,16,256]{2,1,0:T(8,128)S(1)} %get-tuple-element.12.masks, ...), custom_call_target="tpu_custom_call" | custom-call | flops 100000000 | bytes 4000000 | tf_op jit(solution)/shard_map/pallas_call | solution.py:336

commit v4 on v3

--- a/solution.py
+++ b/solution.py
@@ -9,7 +9,7 @@
 
 MESH = pl.DeviceIdType.MESH
 GROUP = 8
-CHUNKS = 4
+CHUNKS = 1
 SLAB = 16
 DEPTH = 12
 LIMIT = 40 * 1024 * 1024
@@ -31,6 +31,10 @@
     half = ref.shape[-1]
     ref[0, at, :] = value[:, :half]
     ref[1, at, :] = value[:, half:]
+
+
+def wrapped(i, n):
+    return jnp.where(i < 0, i + n, jnp.where(i >= n, i - n, i))
 
 
 def one_hot(index, count):
@@ -57,58 +61,15 @@
     ready, load_sem, edge_send, edge_recv, term_send, term_recv,
 ):
     comp, tile = lax.axis_index("comp"), lax.axis_index("tile")
-    partner = lax.rem(comp + n_comp // 2, n_comp)
+    partner = jnp.where(comp < n_comp // 2, comp + n_comp // 2, comp - n_comp // 2)
     rows, cols = coef.shape
     levels = field.shape[1] // rows
     lanes = field.shape[2]
     shift = cols.bit_length() - 1
-    below = (comp, lax.rem(tile + n_tile - 1, n_tile))
-    above = (comp, lax.rem(tile + 1, n_tile))
-    others = [(partner, lax.rem(tile + n_tile + j - entries // 2, n_tile)) for j in range(entries)]
-
-    half = n_tile // 2
-    deep = min(DEPTH, half)
-    wide_by = half // deep
-    x, z, y = lax.rem(lax.div(tile, deep), wide_by), lax.rem(tile, deep), 2 * lax.div(comp, 2) + lax.div(tile, half)
-
-    def rank(offset, across):
-        over, under = z + offset >= deep, z + offset < 0
-        z_there = z + offset + jnp.where(under, deep, 0) - jnp.where(over, deep, 0)
-        x_there = x + jnp.where(over, 1, 0) - jnp.where(under, 1, 0)
-        turn = jnp.logical_or(x_there == wide_by, x_there < 0)
-        x_there = jnp.where(turn, jnp.where(over, 0, wide_by - 1), x_there)
-        y_there = jnp.where(turn, y + 1 - 2 * lax.rem(y, 2), y)
-        if across:
-            y_there = lax.rem(y_there + n_comp // 2, n_comp)
-        when = 13 * jnp.minimum(z_there, 7) + 4 * jnp.maximum(z_there - 7, 0) + 4 * x_there
-        when = when + jnp.where(y_there < 4, 6 * y_there, 42 - 3 * y_there)
-        to_tile = lax.rem(tile + n_tile + offset, n_tile)
-        return (when * n_comp + (partner if across else comp)) * n_tile + to_tile
-
-    own = rank(0, False)
-
-    def after(offset, across):
-        return rank(offset, across) > own
-
-    peers = {}
-    for j in range(entries):
-        offset = j - entries // 2
-        peers["term", offset] = (others[j], after(offset, True), j, entries - 1 - j, j)
-    peers["edge", -1] = (below, after(-1, False), 0, 1, entries)
-    peers["edge", 1] = (above, after(1, False), 1, 0, entries + 1)
-    order = [("term", 0), ("edge", 1), ("term", 1), ("term", 2), ("edge", -1), ("term", -2), ("term", -1)]
-
-    sends = [("term", 1), ("term", 2), ("term", -2), ("term", -1), ("term", 0), ("edge", 1), ("edge", -1)]
-    barrier = pltpu.get_barrier_semaphore()
-    before = 0
-    for key in order:
-        device, is_after = peers[key][:2]
-
-        @pl.when(is_after)
-        def _(device=device):
-            pl.semaphore_signal(barrier, inc=1, device_id=device, device_id_type=MESH)
-
-        before = before + jnp.where(is_after, 0, 1)
+    reach = entries // 2
+    tiles = {o: wrapped(tile + o, n_tile) for o in range(-reach, reach + 1)}
+    below, above = (comp, tiles[-1]), (comp, tiles[1])
+    others = [(partner, tiles[j - reach]) for j in range(entries)]
 
     size = field.shape[1] // CHUNKS
     per_var = field.shape[1] // nvars
@@ -126,6 +87,52 @@
     for copy in copies:
         copy.start()
 
+    half = n_tile // 2
+    deep = min(DEPTH, half)
+    wide_by = half // deep
+    y_low = jnp.where(tile >= half, 1, 0)
+    rest = tile - half * y_low
+    x = sum(jnp.where(rest >= deep * i, 1, 0) for i in range(1, wide_by)) if wide_by > 1 else 0
+    z = rest - deep * x
+    y_high = comp >> 1
+    y_across = partner >> 1
+
+    def rank(offset, across):
+        over, under = z + offset >= deep, z + offset < 0
+        z_there = wrapped(z + offset, deep)
+        x_there = x + jnp.where(over, 1, 0) - jnp.where(under, 1, 0)
+        turn = jnp.logical_or(x_there >= wide_by, x_there < 0)
+        x_there = wrapped(x_there, wide_by)
+        y_there = 2 * (y_across if across else y_high) + jnp.where(turn, 1 - y_low, y_low)
+        when = 4 * z_there + 9 * jnp.minimum(z_there, 7) + 4 * x_there
+        when = when + jnp.where(y_there < 4, 6 * y_there, 42 - 3 * y_there)
+        return (when * n_comp + (partner if across else comp)) * n_tile + tiles[offset]
+
+    own = rank(0, False)
+
+    def after(offset, across):
+        return rank(offset, across) > own
+
+    peers = {}
+    for j in range(entries):
+        offset = j - entries // 2
+        peers["term", offset] = (others[j], after(offset, True), j, entries - 1 - j, j)
+    peers["edge", -1] = (below, after(-1, False), 0, 1, entries)
+    peers["edge", 1] = (above, after(1, False), 1, 0, entries + 1)
+    order = [("term", 0), ("edge", 1), ("term", 1), ("term", 2), ("edge", -1), ("term", -2), ("term", -1)]
+
+    sends = [("term", 1), ("term", 2), ("term", -2), ("term", -1), ("term", 0), ("edge", 1), ("edge", -1)]
+    barrier = pltpu.get_barrier_semaphore()
+    before = 0
+    for key in order:
+        device, is_after = peers[key][:2]
+
+        @pl.when(is_after)
+        def _(device=device):
+            pl.semaphore_signal(barrier, inc=1, device_id=device, device_id_type=MESH)
+
+        before = before + jnp.where(is_after, 0, 1)
+
     @pl.when(before > 0)
     def _():
         pl.semaphore_wait(barrier, before)
@@ -146,8 +153,26 @@
     head = [x.astype(jnp.bfloat16) for x in flux]
     tail = [(x - y.astype(jnp.float32)).astype(jnp.bfloat16) for x, y in zip(flux, head, strict=True)]
     both = jnp.concatenate([jnp.concatenate(head, axis=0), jnp.concatenate(tail, axis=0)], axis=1)
+    def to(key):
+        device, _, out_slot = peers[key][:3]
+        here, there, done, came = (
+            (term_out, term_in, term_send, term_recv) if key[0] == "term" else (edge_out, edge_in, edge_send, edge_recv)
+        )
+        return pltpu.make_async_remote_copy(
+            src_ref=here.at[out_slot], dst_ref=there.at[out_slot], send_sem=done.at[out_slot], recv_sem=came.at[out_slot],
+            device_id=device, device_id_type=MESH,
+        )
+
+    def arrived(key):
+        slot_in = peers[key][3]
+        there, done, came = (term_in, term_send, term_recv) if key[0] == "term" else (edge_in, edge_send, edge_recv)
+        pltpu.make_async_remote_copy(
+            src_ref=there.at[slot_in], dst_ref=there.at[slot_in], send_sem=done.at[slot_in], recv_sem=came.at[slot_in],
+            device_id=peers[key][0], device_id_type=MESH,
+        ).wait_recv()
+
     slot = lax.broadcasted_iota(jnp.int32, (1, slots), 1)
-    for j in range(entries):
+    def compute(j):
         index = src_v[j]
         column = one_hot(index & (cols - 1), cols).astype(jnp.bfloat16)
         weight = jnp.where(slot < count_s[0, j], inter_v[j], 0.0)
@@ -158,29 +183,14 @@
             [picked, jnp.zeros((term_out.shape[1] - nf, slots), jnp.float32)], axis=0
         ).astype(jnp.bfloat16)
 
-    def to(key):
-        device, _, out_slot = peers[key][:3]
-        here, there, done, came = (
-            (term_out, term_in, term_send, term_recv) if key[0] == "term" else (edge_out, edge_in, edge_send, edge_recv)
-        )
-        return pltpu.make_async_remote_copy(
-            src_ref=here.at[out_slot], dst_ref=there.at[out_slot], send_sem=done.at[out_slot], recv_sem=came.at[out_slot],
-            device_id=device, device_id_type=MESH,
-        )
-
-    def arrived(key):
-        slot_in = peers[key][3]
-        there, done, came = (term_in, term_send, term_recv) if key[0] == "term" else (edge_in, edge_send, edge_recv)
-        pltpu.make_async_remote_copy(
-            src_ref=there.at[slot_in], dst_ref=there.at[slot_in], send_sem=done.at[slot_in], recv_sem=came.at[slot_in],
-            device_id=peers[key][0], device_id_type=MESH,
-        ).wait_recv()
-
-    for key in sends[:entries]:
-
-        @pl.when(jnp.logical_not(peers[key][1]))
-        def _(key=key):
-            to(key).start()
+    for group in (sends[:2], sends[2:entries]):
+        for key in group:
+            compute(peers[key][2])
+        for key in group:
+
+            @pl.when(jnp.logical_not(peers[key][1]))
+            def _(key=key):
+                to(key).start()
 
     for copy in middle:
         copy.wait()
@@ -217,13 +227,19 @@
         masks[j, :, :] = one_hot(dst_v[j] >> shift, rows)
     inverse[...] = 1.0 / cell[...]
 
-    for key in order:
-
-        @pl.when(peers[key][1])
-        def _(key=key):
+    near = [("term", -2), ("term", -1), ("edge", -1), ("edge", 1), ("term", 0), ("term", 1), ("term", 2)]
+    for wraps, keys in ((False, near), (True, [("edge", -1), ("term", -2), ("term", -1)])):
+        for key in keys:
             kind, offset = key
-            pl.semaphore_wait(ready.at[peers[kind, -offset][4]], 1)
-            to(key).start()
+            due = peers[key][1]
+            if offset < 0:
+                under = z + offset < 0
+                due = jnp.logical_and(due, under if wraps else jnp.logical_not(under))
+
+            @pl.when(due)
+            def _(key=key, kind=kind, offset=offset):
+                pl.semaphore_wait(ready.at[peers[kind, -offset][4]], 1)
+                to(key).start()
 
     arrived(("edge", 1))
     arrived(("edge", -1))

time: 26.8 us -> 26.8 us (level)
  the two profiles are of different devices: /device:TPU:1 before, /device:TPU:16 now
where the time goes in v4:
time: 26.8 us; the launch traced here: 26.6 us
  Pallas kernels  26 us (97%)
  between operations  0.64 us (2%)
    pallas_call x1, Pallas kernels, local(): pl.pallas_call(functools.partial(kernel, n_comp, n_tile, nvars, nf, entri...  24.7 us
    pallas_call x1, Pallas kernels, local(): pl.pallas_call(functools.partial(finish_kernel, nvars, nf, entries, slots...  1.24 us

profile of v4, /device:TPU:16, one launch (start us, length us, event | category | flops | bytes accessed | tf_op | source)
XLA Modules:
  0.0 26.6 jit_solution(3350752306037882236)
XLA Ops:
  0.6 24.7 %shard_map.104 = (f32[2,1536,128]{2,1,0:T(8,128)S(1)}, bf16[5,16,256]{2,1,0:T(8,128)(2,1)S(1)}, bf16[1280,256]{1,0:T(8,128)(2,1)S(1)}, f32[5,16,256]{2,1,0:T(8,128)S(1)}, f32[16,256]{1,0:T(8,128)S(1)}) custom-call(f32[1536,256]{1,0:T(8,128)} %bitcast.10, f32[16,256]{1,0:T(8,128)} %bitcast.12, f32[192,256]{1,0:T(8,128)} %bitcast.11, f32[1,12]{1,0:T(1,128)} %gain.1, ...), custom_call_target="tpu_custom_call" | custom-call | flops 100000000 | bytes 4000000 | tf_op jit(solution)/shard_map/pallas_call | solution.py:300
  25.4 1.2 %shard_map.105 = (f32[1536,256]{1,0:T(8,128)}, f32[192,256]{1,0:T(8,128)}) custom-call(f32[2,1536,128]{2,1,0:T(8,128)S(1)} %get-tuple-element.9.result, bf16[5,16,256]{2,1,0:T(8,128)(2,1)S(1)} %get-tuple-element.10.term_in, bf16[1280,256]{1,0:T(8,128)(2,1)S(1)} %get-tuple-element.11.spread, f32[5,16,256]{2,1,0:T(8,128)S(1)} %get-tuple-element.12.masks, ...), custom_call_target="tpu_custom_call" | custom-call | flops 100000000 | bytes 4000000 | tf_op jit(solution)/shard_map/pallas_call | solution.py:352

commit v5 on v4

--- a/solution.py
+++ b/solution.py
@@ -105,7 +105,7 @@
         x_there = wrapped(x_there, wide_by)
         y_there = 2 * (y_across if across else y_high) + jnp.where(turn, 1 - y_low, y_low)
         when = 4 * z_there + 9 * jnp.minimum(z_there, 7) + 4 * x_there
-        when = when + jnp.where(y_there < 4, 6 * y_there, 42 - 3 * y_there)
+        when = when + jnp.where(y_there < 4, 6 * y_there, 54 - 3 * y_there)
         return (when * n_comp + (partner if across else comp)) * n_tile + tiles[offset]
 
     own = rank(0, False)
@@ -183,7 +183,7 @@
             [picked, jnp.zeros((term_out.shape[1] - nf, slots), jnp.float32)], axis=0
         ).astype(jnp.bfloat16)
 
-    for group in (sends[:2], sends[2:entries]):
+    def leave(group):
         for key in group:
             compute(peers[key][2])
         for key in group:
@@ -192,6 +192,7 @@
             def _(key=key):
                 to(key).start()
 
+    leave(sends[:2])
     for copy in middle:
         copy.wait()
     for side, (near, far) in enumerate(((0, 1), (rows - 1, rows - 2))):
@@ -204,6 +205,8 @@
         @pl.when(jnp.logical_not(peers[key][1]))
         def _(key=key):
             to(key).start()
+
+    leave(sends[2:entries])
 
     row = lax.broadcasted_iota(jnp.int32, (GROUP, 8, cols), 1)
     first, last = row == 0, row == 7

time: 26.8 us -> 26.6 us (level)
  the two profiles are of different devices: /device:TPU:16 before, /device:TPU:1 now
where the time goes in v5:
time: 26.6 us; the launch traced here: 26.2 us
  Pallas kernels  25.6 us (96%)
  between operations  0.64 us (2%)
    pallas_call x1, Pallas kernels, local(): pl.pallas_call(functools.partial(kernel, n_comp, n_tile, nvars, nf, entri...  24.3 us
    pallas_call x1, Pallas kernels, local(): pl.pallas_call(functools.partial(finish_kernel, nvars, nf, entries, slots...  1.24 us

profile of v5, /device:TPU:1, one launch (start us, length us, event | category | flops | bytes accessed | tf_op | source)
XLA Modules:
  0.0 26.2 jit_solution(6938676570768941064)
XLA Ops:
  0.6 24.3 %shard_map.104 = (f32[2,1536,128]{2,1,0:T(8,128)S(1)}, bf16[5,16,256]{2,1,0:T(8,128)(2,1)S(1)}, bf16[1280,256]{1,0:T(8,128)(2,1)S(1)}, f32[5,16,256]{2,1,0:T(8,128)S(1)}, f32[16,256]{1,0:T(8,128)S(1)}) custom-call(f32[1536,256]{1,0:T(8,128)} %bitcast.10, f32[16,256]{1,0:T(8,128)} %bitcast.12, f32[192,256]{1,0:T(8,128)} %bitcast.11, f32[1,12]{1,0:T(1,128)} %gain.1, ...), custom_call_target="tpu_custom_call" | custom-call | flops 100000000 | bytes 4000000 | tf_op jit(solution)/shard_map/pallas_call | solution.py:303
  25.0 1.2 %shard_map.105 = (f32[1536,256]{1,0:T(8,128)}, f32[192,256]{1,0:T(8,128)}) custom-call(f32[2,1536,128]{2,1,0:T(8,128)S(1)} %get-tuple-element.9.result, bf16[5,16,256]{2,1,0:T(8,128)(2,1)S(1)} %get-tuple-element.10.term_in, bf16[1280,256]{1,0:T(8,128)(2,1)S(1)} %get-tuple-element.11.spread, f32[5,16,256]{2,1,0:T(8,128)S(1)} %get-tuple-element.12.masks, ...), custom_call_target="tpu_custom_call" | custom-call | flops 100000000 | bytes 4000000 | tf_op jit(solution)/shard_map/pallas_call | solution.py:355

commit v6 on v5

--- a/solution.py
+++ b/solution.py
@@ -244,9 +244,8 @@
                 pl.semaphore_wait(ready.at[peers[kind, -offset][4]], 1)
                 to(key).start()
 
-    arrived(("edge", 1))
-    arrived(("edge", -1))
-    for side, (near, far) in ((1, (0, 1)), (0, (rows - 1, rows - 2))):
+    for side, (near, far) in ((0, (rows - 1, rows - 2)), (1, (0, 1))):
+        arrived(("edge", 1 if side == 0 else -1))
         k_near, k_far = coef[near:near + 1, :], coef[far:far + 1, :]
         k_out = edge_in[side, 2 * levels:, :].astype(jnp.float32)[0:1, :]
         for g in range(0, levels, SLAB):

time: 26.6 us -> 26.6 us (level)
  no operation moved by 1% of the time
where the time goes in v6:
time: 26.6 us; the launch traced here: 26.2 us
  Pallas kernels  25.6 us (96%)
  between operations  0.64 us (2%)
    pallas_call x1, Pallas kernels, local(): pl.pallas_call(functools.partial(kernel, n_comp, n_tile, nvars, nf, entri...  24.3 us
    pallas_call x1, Pallas kernels, local(): pl.pallas_call(functools.partial(finish_kernel, nvars, nf, entries, slots...  1.24 us

profile of v6, /device:TPU:1, one launch (start us, length us, event | category | flops | bytes accessed | tf_op | source)
XLA Modules:
  0.0 26.2 jit_solution(4139456925793315591)
XLA Ops:
  0.6 24.3 %shard_map.104 = (f32[2,1536,128]{2,1,0:T(8,128)S(1)}, bf16[5,16,256]{2,1,0:T(8,128)(2,1)S(1)}, bf16[1280,256]{1,0:T(8,128)(2,1)S(1)}, f32[5,16,256]{2,1,0:T(8,128)S(1)}, f32[16,256]{1,0:T(8,128)S(1)}) custom-call(f32[1536,256]{1,0:T(8,128)} %bitcast.10, f32[16,256]{1,0:T(8,128)} %bitcast.12, f32[192,256]{1,0:T(8,128)} %bitcast.11, f32[1,12]{1,0:T(1,128)} %gain.1, ...), custom_call_target="tpu_custom_call" | custom-call | flops 100000000 | bytes 4000000 | tf_op jit(solution)/shard_map/pallas_call | solution.py:302
  25.0 1.2 %shard_map.105 = (f32[1536,256]{1,0:T(8,128)}, f32[192,256]{1,0:T(8,128)}) custom-call(f32[2,1536,128]{2,1,0:T(8,128)S(1)} %get-tuple-element.9.result, bf16[5,16,256]{2,1,0:T(8,128)(2,1)S(1)} %get-tuple-element.10.term_in, bf16[1280,256]{1,0:T(8,128)(2,1)S(1)} %get-tuple-element.11.spread, f32[5,16,256]{2,1,0:T(8,128)S(1)} %get-tuple-element.12.masks, ...), custom_call_target="tpu_custom_call" | custom-call | flops 100000000 | bytes 4000000 | tf_op jit(solution)/shard_map/pallas_call | solution.py:354
